TPU v7x, 32 devices: a whole 2x2x4 slice. The times are simulated.
32 devices in a mesh: lat: 2 (over x), lon: 16 (over z, y, core).
Axes of the slice: x: 2, y: 2, z: 4, core: 2. Of those that a mesh axis runs over, the one named last changes fastest.
Arguments:
- ocean_field: bfloat16 [32, 256, 256], P('lat', 'lon'), may hold values from -6 to 6
- ocean_mask: int32 [32, 256], P('lat', 'lon'), may hold values from 0 to 1, as said below
- kernels: float32 [4, 7, 7, 256], replicated, may hold values from -0.875 to 0.875
- gains: float32 [4, 256], replicated, may hold values from 0.1 to 1.9
- w_in: bfloat16 [4, 256, 1024], replicated, may hold values from -0.375 to 0.375
- b_in: float32 [4, 1024], replicated, may hold values from -6 to 6
- w_out: bfloat16 [4, 1024, 256], replicated, may hold values from -0.1875 to 0.1875
Outputs:
- new_field: bfloat16 [32, 256, 256], P('lat', 'lon')
Inputs may be any that keep to these rules, and one draw needn't show every extreme that they name: `ocean_mask`: each device's tile of 16 x 16 cells holds at most 192 wet cells; some tile holds exactly 192, and some tiles hold none.
All inputs are finite; a program needn't handle non-finite values.
Results may differ from a plain program's by a relative error of at most 0.0095.
Values may be sent and summed in bfloat16 or wider, within the bound.
A program may use at most 64 MiB of HBM per device.

v0:
```python
import jax
import jax.numpy as jnp
from jax import lax
from jax.sharding import PartitionSpec as P


def padded_2(cells, sides, width, closed):
    for axis, dim in sides:
        count = lax.axis_size(axis)
        ends = count if closed else count - 1
        head = lax.slice_in_dim(cells, 0, width, axis=dim)
        tail = lax.slice_in_dim(cells, cells.shape[dim] - width, cells.shape[dim], axis=dim)
        cells = jnp.concatenate(
            [
                lax.ppermute(tail, axis, [(i, (i + 1) % count) for i in range(ends)]),
                cells,
                lax.ppermute(head, axis, [((i + 1) % count, i) for i in range(ends)]),
            ],
            axis=dim,
        )
    return cells


def cos_rows(row_start, row_count, total_rows):
    globe_rows = row_start + jnp.arange(row_count, dtype=jnp.int32)
    latitude = jnp.pi * ((globe_rows.astype(jnp.float32) + 0.5) / total_rows - 0.5)
    inside = (globe_rows >= 0) & (globe_rows < total_rows)
    return jnp.where(inside, jnp.cos(latitude), jnp.float32(0.0))


def metric_conv(padded, kernel, row_cos):
    out_rows = padded.shape[0] - 6
    out_cols = padded.shape[1] - 6
    scaled = padded.astype(jnp.float32) * row_cos[:, None, None]
    summed = jnp.zeros((out_rows, out_cols, padded.shape[2]), jnp.float32)
    for a in range(7):
        for b in range(7):
            summed = summed + kernel[a, b] * scaled[a : a + out_rows, b : b + out_cols]
    row_weight = row_cos[0:out_rows]
    for a in range(1, 7):
        row_weight = row_weight + row_cos[a : a + out_rows]
    return summed * (7.0 / row_weight)[:, None, None]


def mixer_rows(stencil_rows, gain_vec, w_first, b_first, w_second):
    mean_square = jnp.mean(stencil_rows * stencil_rows, axis=-1, keepdims=True)
    normed = (stencil_rows * lax.rsqrt(mean_square + 1e-06) * gain_vec).astype(jnp.bfloat16)
    hidden = jax.nn.silu(
        jnp.dot(normed, w_first, preferred_element_type=jnp.float32) + b_first
    ).astype(jnp.bfloat16)
    return jnp.dot(hidden, w_second, preferred_element_type=jnp.float32)


def dense_mix(state_now, stencil, wet_mask, gain_vec, w_first, b_first, w_second):
    channels = state_now.shape[-1]
    update = mixer_rows(
        stencil.reshape(-1, channels), gain_vec, w_first, b_first, w_second
    ).reshape(stencil.shape)
    return (
        (state_now.astype(jnp.float32) + update) * wet_mask[..., None].astype(jnp.float32)
    ).astype(jnp.bfloat16)


def own_mix(state_now, stencil, wet_mask, gain_vec, w_first, b_first, w_second):
    return dense_mix(state_now, stencil, wet_mask, gain_vec, w_first, b_first, w_second)


def local(ocean_field, ocean_mask, kernels, gains, w_in, b_in, w_out):
    tile_rows = ocean_field.shape[0]
    total_rows = tile_rows * lax.axis_size("lat")
    row_start = lax.axis_index("lat") * tile_rows
    layer_total = kernels.shape[0]
    state_now = ocean_field
    cos_near = cos_rows(row_start - 3, tile_rows + 6, total_rows)
    for layer_index in range(layer_total):
        padded = padded_2(state_now, (("lat", 0),), 3, False)
        padded = padded_2(padded, (("lon", 1),), 3, True)
        stencil = metric_conv(padded, kernels[layer_index], cos_near)
        state_now = own_mix(
            state_now,
            stencil,
            ocean_mask,
            gains[layer_index],
            w_in[layer_index],
            b_in[layer_index],
            w_out[layer_index],
        )
    return state_now


def solution(mesh):
    in_specs = (P("lat", "lon", None), P("lat", "lon"), P(), P(), P(), P(), P())
    out_specs = P("lat", "lon", None)
    return jax.shard_map(local, mesh=mesh, in_specs=in_specs, out_specs=out_specs, check_vma=False)
```

profile of v0, /device:TPU:0, one launch (start us, length us, event | category | flops | bytes accessed | tf_op | source)
XLA Modules:
  0.0 72.3 jit_solution(10577611585803085723)
XLA Ops:
  0.8 1.3 %collective-permute-start.1 = (bf16[3,16,256]{2,1,0:T(8,128)(2,1)S(1)}, bf16[3,16,256]{2,1,0:T(8,128)(2,1)S(1)}, u32[]{:S(2)}, u32[]{:S(2)}) collective-permute-start(bf16[3,16,256]{2,1,0:T(8,128)(2,1)S(1)} %get-tuple-element.31), channel_id=1, source_target_pairs={{16,0},{17,1},{18,2},{19,3},{20,4},{21,5},{22,6},{23,7},{24,8},{25... | collective-permute-start | bytes 73736 | tf_op jit(solution)/shard_map/ppermute | solution.py:17
  2.0 4.8 %collective-permute-start = (bf16[3,16,256]{2,1,0:T(8,128)(2,1)S(1)}, bf16[3,16,256]{2,1,0:T(8,128)(2,1)S(1)}, u32[]{:S(2)}, u32[]{:S(2)}) collective-permute-start(bf16[3,16,256]{2,1,0:T(8,128)(2,1)S(1)} %get-tuple-element.32), channel_id=1, source_target_pairs={{0,16},{1,17},{2,18},{3,19},{4,20},{5,21},{6,22},{7,23},{8,24},{9,... | collective-permute-start | bytes 73736 | tf_op jit(solution)/shard_map/ppermute | solution.py:15
  6.9 1.5 %fusion.224 = (f32[1,7,7,256]{3,0,2,1:T(1,128)S(1)}, f32[1,7,7,256]{3,0,2,1:T(1,128)S(1)}, f32[1,7,7,256]{3,0,2,1:T(1,128)S(1)}, f32[1,7,7,256]{3,0,2,1:T(1,128)S(1)}) fusion(f32[4,7,7,256]{3,0,2,1:T(4,128)} %param.9), kind=kLoop, calls=%fused_computation.462 | loop fusion | bytes 401408 | tf_op jit(solution)/shard_map/slice | solution.py:78
  11.5 4.6 %collective-permute-start.3 = (bf16[22,3,256]{2,1,0:T(4,128)(2,1)S(1)}, bf16[22,3,256]{2,1,0:T(4,128)(2,1)S(1)}, u32[]{:S(2)}, u32[]{:S(2)}) collective-permute-start(bf16[22,3,256]{2,1,0:T(4,128)(2,1)S(1)} %get-tuple-element.24), channel_id=1, source_target_pairs={{1,0},{2,1},{3,2},{4,3},{5,4},{6,5},{7,6},{8,7},{9,8},{10,9},{11,1... | collective-permute-start | bytes 101384 | tf_op jit(solution)/shard_map/ppermute | solution.py:17
  18.0 1.8 %multiply_reduce_fusion.3 = (f32[16,16]{1,0:T(8,128)S(1)}, f32[16,16,256]{2,1,0:T(8,128)S(1)}) fusion(f32[16]{0:T(128)S(1)} %add_divide_fusion, f32[22,22,256]{2,1,0:T(8,128)S(1)} %convert_multiply_fusion.3, f32[256]{0:T(256)S(1)} %bitcast.367, f32[256]{0:T(256)S(1)} %bitcast.368, f32[256]{0:T(256)S(1)} %bitcast.369, f32[256]{0:T(256)S(1)} %bitcast.370, ...), kind=kLoop, calls=%fused_computation.439 | loop fusion | flops 6553344 | bytes 13158464 | tf_op jit(solution)/shard_map/reduce_sum | solution.py:46
  21.9 2.0 %collective-permute-start.4 = (bf16[3,16,256]{2,1,0:T(8,128)(2,1)S(1)}, bf16[3,16,256]{2,1,0:T(8,128)(2,1)S(1)}, u32[]{:S(2)}, u32[]{:S(2)}) collective-permute-start(bf16[3,16,256]{2,1,0:T(8,128)(2,1)S(1)} %get-tuple-element.29), channel_id=1, source_target_pairs={{0,16},{1,17},{2,18},{3,19},{4,20},{5,21},{6,22},{7,23},{8,24},{9,... | collective-permute-start | bytes 73736 | tf_op jit(solution)/shard_map/ppermute | solution.py:15
  23.9 1.3 %collective-permute-start.5 = (bf16[3,16,256]{2,1,0:T(8,128)(2,1)S(1)}, bf16[3,16,256]{2,1,0:T(8,128)(2,1)S(1)}, u32[]{:S(2)}, u32[]{:S(2)}) collective-permute-start(bf16[3,16,256]{2,1,0:T(8,128)(2,1)S(1)} %get-tuple-element.30), channel_id=1, source_target_pairs={{16,0},{17,1},{18,2},{19,3},{20,4},{21,5},{22,6},{23,7},{24,8},{25... | collective-permute-start | bytes 73736 | tf_op jit(solution)/shard_map/ppermute | solution.py:17
  25.4 4.2 %collective-permute-done.5 = bf16[3,16,256]{2,1,0:T(8,128)(2,1)S(1)} collective-permute-done((bf16[3,16,256]{2,1,0:T(8,128)(2,1)S(1)}, bf16[3,16,256]{2,1,0:T(8,128)(2,1)S(1)}, u32[]{:S(2)}, u32[]{:S(2)}) %collective-permute-start.5) | collective-permute-done | bytes 24608 | tf_op jit(solution)/shard_map/ppermute | solution.py:17
  29.8 4.4 %collective-permute-start.7 = (bf16[22,3,256]{2,1,0:T(4,128)(2,1)S(1)}, bf16[22,3,256]{2,1,0:T(4,128)(2,1)S(1)}, u32[]{:S(2)}, u32[]{:S(2)}) collective-permute-start(bf16[22,3,256]{2,1,0:T(4,128)(2,1)S(1)} %get-tuple-element.22), channel_id=1, source_target_pairs={{1,0},{2,1},{3,2},{4,3},{5,4},{6,5},{7,6},{8,7},{9,8},{10,9},{11,1... | collective-permute-start | bytes 101384 | tf_op jit(solution)/shard_map/ppermute | solution.py:17
  34.2 1.7 %collective-permute-done.6 = bf16[22,3,256]{2,1,0:T(4,128)(2,1)S(1)} collective-permute-done((bf16[22,3,256]{2,1,0:T(4,128)(2,1)S(1)}, bf16[22,3,256]{2,1,0:T(4,128)(2,1)S(1)}, u32[]{:S(2)}, u32[]{:S(2)}) %collective-permute-start.6) | collective-permute-done | bytes 33824 | tf_op jit(solution)/shard_map/ppermute | solution.py:15
  36.0 1.8 %multiply_reduce_fusion.2 = (f32[16,16]{1,0:T(8,128)S(1)}, f32[16,16,256]{2,1,0:T(8,128)S(1)}) fusion(f32[16]{0:T(128)S(1)} %add_divide_fusion, f32[22,22,256]{2,1,0:T(8,128)S(1)} %convert_multiply_fusion.2, f32[256]{0:T(256)S(1)} %bitcast.405, f32[256]{0:T(256)S(1)} %bitcast.406, f32[256]{0:T(256)S(1)} %bitcast.407, f32[256]{0:T(256)S(1)} %bitcast.408, ...), kind=kLoop, calls=%fused_computation.437 | loop fusion | flops 6553344 | bytes 13158464 | tf_op jit(solution)/shard_map/reduce_sum | solution.py:46
  38.8 1.6 %collective-permute-start.8 = (bf16[3,16,256]{2,1,0:T(8,128)(2,1)S(1)}, bf16[3,16,256]{2,1,0:T(8,128)(2,1)S(1)}, u32[]{:S(2)}, u32[]{:S(2)}) collective-permute-start(bf16[3,16,256]{2,1,0:T(8,128)(2,1)S(1)} %get-tuple-element.27), channel_id=1, source_target_pairs={{0,16},{1,17},{2,18},{3,19},{4,20},{5,21},{6,22},{7,23},{8,24},{9,... | collective-permute-start | bytes 73736 | tf_op jit(solution)/shard_map/ppermute | solution.py:15
  40.4 1.3 %collective-permute-start.9 = (bf16[3,16,256]{2,1,0:T(8,128)(2,1)S(1)}, bf16[3,16,256]{2,1,0:T(8,128)(2,1)S(1)}, u32[]{:S(2)}, u32[]{:S(2)}) collective-permute-start(bf16[3,16,256]{2,1,0:T(8,128)(2,1)S(1)} %get-tuple-element.28), channel_id=1, source_target_pairs={{16,0},{17,1},{18,2},{19,3},{20,4},{21,5},{22,6},{23,7},{24,8},{25... | collective-permute-start | bytes 73736 | tf_op jit(solution)/shard_map/ppermute | solution.py:17
  41.9 4.2 %collective-permute-done.9 = bf16[3,16,256]{2,1,0:T(8,128)(2,1)S(1)} collective-permute-done((bf16[3,16,256]{2,1,0:T(8,128)(2,1)S(1)}, bf16[3,16,256]{2,1,0:T(8,128)(2,1)S(1)}, u32[]{:S(2)}, u32[]{:S(2)}) %collective-permute-start.9) | collective-permute-done | bytes 24608 | tf_op jit(solution)/shard_map/ppermute | solution.py:17
  46.2 4.4 %collective-permute-start.11 = (bf16[22,3,256]{2,1,0:T(4,128)(2,1)S(1)}, bf16[22,3,256]{2,1,0:T(4,128)(2,1)S(1)}, u32[]{:S(2)}, u32[]{:S(2)}) collective-permute-start(bf16[22,3,256]{2,1,0:T(4,128)(2,1)S(1)} %get-tuple-element.20), channel_id=1, source_target_pairs={{1,0},{2,1},{3,2},{4,3},{5,4},{6,5},{7,6},{8,7},{9,8},{10,9},{11,1... | collective-permute-start | bytes 101384 | tf_op jit(solution)/shard_map/ppermute | solution.py:17
  50.7 1.7 %collective-permute-done.10 = bf16[22,3,256]{2,1,0:T(4,128)(2,1)S(1)} collective-permute-done((bf16[22,3,256]{2,1,0:T(4,128)(2,1)S(1)}, bf16[22,3,256]{2,1,0:T(4,128)(2,1)S(1)}, u32[]{:S(2)}, u32[]{:S(2)}) %collective-permute-start.10) | collective-permute-done | bytes 33824 | tf_op jit(solution)/shard_map/ppermute | solution.py:15
  52.5 1.8 %multiply_reduce_fusion.1 = (f32[16,16]{1,0:T(8,128)S(1)}, f32[16,16,256]{2,1,0:T(8,128)S(1)}) fusion(f32[16]{0:T(128)S(1)} %add_divide_fusion, f32[22,22,256]{2,1,0:T(8,128)S(1)} %convert_multiply_fusion.1, f32[256]{0:T(256)S(1)} %bitcast.280, f32[256]{0:T(256)S(1)} %bitcast.281, f32[256]{0:T(256)S(1)} %bitcast.282, f32[256]{0:T(256)S(1)} %bitcast.283, ...), kind=kLoop, calls=%fused_computation.435 | loop fusion | flops 6553344 | bytes 13158464 | tf_op jit(solution)/shard_map/reduce_sum | solution.py:46
  55.2 1.6 %collective-permute-start.12 = (bf16[3,16,256]{2,1,0:T(8,128)(2,1)S(1)}, bf16[3,16,256]{2,1,0:T(8,128)(2,1)S(1)}, u32[]{:S(2)}, u32[]{:S(2)}) collective-permute-start(bf16[3,16,256]{2,1,0:T(8,128)(2,1)S(1)} %get-tuple-element.25), channel_id=1, source_target_pairs={{0,16},{1,17},{2,18},{3,19},{4,20},{5,21},{6,22},{7,23},{8,24},{9,... | collective-permute-start | bytes 73736 | tf_op jit(solution)/shard_map/ppermute | solution.py:15
  56.9 1.3 %collective-permute-start.13 = (bf16[3,16,256]{2,1,0:T(8,128)(2,1)S(1)}, bf16[3,16,256]{2,1,0:T(8,128)(2,1)S(1)}, u32[]{:S(2)}, u32[]{:S(2)}) collective-permute-start(bf16[3,16,256]{2,1,0:T(8,128)(2,1)S(1)} %get-tuple-element.26), channel_id=1, source_target_pairs={{16,0},{17,1},{18,2},{19,3},{20,4},{21,5},{22,6},{23,7},{24,8},{25... | collective-permute-start | bytes 73736 | tf_op jit(solution)/shard_map/ppermute | solution.py:17
  58.4 4.2 %collective-permute-done.13 = bf16[3,16,256]{2,1,0:T(8,128)(2,1)S(1)} collective-permute-done((bf16[3,16,256]{2,1,0:T(8,128)(2,1)S(1)}, bf16[3,16,256]{2,1,0:T(8,128)(2,1)S(1)}, u32[]{:S(2)}, u32[]{:S(2)}) %collective-permute-start.13) | collective-permute-done | bytes 24608 | tf_op jit(solution)/shard_map/ppermute | solution.py:17
  62.7 4.4 %collective-permute-start.15 = (bf16[22,3,256]{2,1,0:T(4,128)(2,1)S(1)}, bf16[22,3,256]{2,1,0:T(4,128)(2,1)S(1)}, u32[]{:S(2)}, u32[]{:S(2)}) collective-permute-start(bf16[22,3,256]{2,1,0:T(4,128)(2,1)S(1)} %get-tuple-element.18), channel_id=1, source_target_pairs={{1,0},{2,1},{3,2},{4,3},{5,4},{6,5},{7,6},{8,7},{9,8},{10,9},{11,1... | collective-permute-start | bytes 101384 | tf_op jit(solution)/shard_map/ppermute | solution.py:17
  67.1 1.7 %collective-permute-done.14 = bf16[22,3,256]{2,1,0:T(4,128)(2,1)S(1)} collective-permute-done((bf16[22,3,256]{2,1,0:T(4,128)(2,1)S(1)}, bf16[22,3,256]{2,1,0:T(4,128)(2,1)S(1)}, u32[]{:S(2)}, u32[]{:S(2)}) %collective-permute-start.14) | collective-permute-done | bytes 33824 | tf_op jit(solution)/shard_map/ppermute | solution.py:15
  69.0 1.8 %multiply_reduce_fusion = (f32[16,16]{1,0:T(8,128)S(1)}, f32[16,16,256]{2,1,0:T(8,128)S(1)}) fusion(f32[16]{0:T(128)S(1)} %add_divide_fusion, f32[22,22,256]{2,1,0:T(8,128)S(1)} %convert_multiply_fusion, f32[256]{0:T(256)S(1)} %bitcast.386, f32[256]{0:T(256)S(1)} %bitcast.387, f32[256]{0:T(256)S(1)} %bitcast.388, f32[256]{0:T(256)S(1)} %bitcast.389, ...), kind=kLoop, calls=%fused_computation.433 | loop fusion | flops 6553344 | bytes 13158464 | tf_op jit(solution)/shard_map/reduce_sum | solution.py:46
  71.4 1.0 %fusion.4 = bf16[16,16,256]{2,1,0:T(8,128)(2,1)} fusion(bf16[16,16,1024]{2,1,0:T(8,128)(2,1)S(1)} %bitcast.464, bf16[4,1024,256]{2,1,0:T(8,128)(2,1)S(1)} %copy-done.2, bf16[16,16,256]{2,1,0:T(8,128)(2,1)S(1)} %fusion.5, f32[16,16]{1,0:T(8,128)S(1)} %convert_element_type.92), kind=kOutput, calls=%fused_computation.12 | convolution fusion | flops 134479872 | bytes 1318912 | tf_op jit(solution)/shard_map/dot_general | solution.py:51
  (69 shorter events, 11.3 us)
Async XLA Ops:
  0.8 10.6 %collective-permute-start.1 = (bf16[3,16,256]{2,1,0:T(8,128)(2,1)S(1)}, bf16[3,16,256]{2,1,0:T(8,128)(2,1)S(1)}, u32[]{:S(2)}, u32[]{:S(2)}) collective-permute-start(bf16[3,16,256]{2,1,0:T(8,128)(2,1)S(1)} %get-tuple-element.31), channel_id=1, source_target_pairs={{16,0},{17,1},{18,2},{19,3},{20,4},{21,5},{22,6},{23,7},{24,8},{25... | collective-permute-start | bytes 73736 | tf_op jit(solution)/shard_map/ppermute | solution.py:17
  2.0 8.4 %collective-permute-start = (bf16[3,16,256]{2,1,0:T(8,128)(2,1)S(1)}, bf16[3,16,256]{2,1,0:T(8,128)(2,1)S(1)}, u32[]{:S(2)}, u32[]{:S(2)}) collective-permute-start(bf16[3,16,256]{2,1,0:T(8,128)(2,1)S(1)} %get-tuple-element.32), channel_id=1, source_target_pairs={{0,16},{1,17},{2,18},{3,19},{4,20},{5,21},{6,22},{7,23},{8,24},{9,... | collective-permute-start | bytes 73736 | tf_op jit(solution)/shard_map/ppermute | solution.py:15
  11.4 6.4 %collective-permute-start.2 = (bf16[22,3,256]{2,1,0:T(4,128)(2,1)S(1)}, bf16[22,3,256]{2,1,0:T(4,128)(2,1)S(1)}, u32[]{:S(2)}, u32[]{:S(2)}) collective-permute-start(bf16[22,3,256]{2,1,0:T(4,128)(2,1)S(1)} %get-tuple-element.23), channel_id=1, source_target_pairs={{0,1},{1,2},{2,3},{3,4},{4,5},{5,6},{6,7},{7,8},{8,9},{9,10},{10,1... | collective-permute-start | bytes 101384 | tf_op jit(solution)/shard_map/ppermute | solution.py:15
  11.5 6.4 %collective-permute-start.3 = (bf16[22,3,256]{2,1,0:T(4,128)(2,1)S(1)}, bf16[22,3,256]{2,1,0:T(4,128)(2,1)S(1)}, u32[]{:S(2)}, u32[]{:S(2)}) collective-permute-start(bf16[22,3,256]{2,1,0:T(4,128)(2,1)S(1)} %get-tuple-element.24), channel_id=1, source_target_pairs={{1,0},{2,1},{3,2},{4,3},{5,4},{6,5},{7,6},{8,7},{9,8},{10,9},{11,1... | collective-permute-start | bytes 101384 | tf_op jit(solution)/shard_map/ppermute | solution.py:17
  18.0 1.9 %copy-start.1 = (bf16[4,256,1024]{2,1,0:T(8,128)(2,1)S(1)}, bf16[4,256,1024]{2,1,0:T(8,128)(2,1)}, u32[]{:S(2)}) copy-start(bf16[4,256,1024]{2,1,0:T(8,128)(2,1)} %param.11) | copy-start | bytes 6291460
  19.9 0.9 %copy-start = (bf16[16,16,256]{2,1,0:T(8,128)(2,1)S(1)}, bf16[16,16,256]{2,1,0:T(8,128)(2,1)}, u32[]{:S(2)}) copy-start(bf16[16,16,256]{2,1,0:T(8,128)(2,1)} %param.7) | copy-start | bytes 393220
  19.9 1.7 %copy-start.2 = (bf16[4,1024,256]{2,1,0:T(8,128)(2,1)S(1)}, bf16[4,1024,256]{2,1,0:T(8,128)(2,1)}, u32[]{:S(2)}) copy-start(bf16[4,1024,256]{2,1,0:T(8,128)(2,1)} %param.13) | copy-start | bytes 6291460
  21.9 3.5 %collective-permute-start.4 = (bf16[3,16,256]{2,1,0:T(8,128)(2,1)S(1)}, bf16[3,16,256]{2,1,0:T(8,128)(2,1)S(1)}, u32[]{:S(2)}, u32[]{:S(2)}) collective-permute-start(bf16[3,16,256]{2,1,0:T(8,128)(2,1)S(1)} %get-tuple-element.29), channel_id=1, source_target_pairs={{0,16},{1,17},{2,18},{3,19},{4,20},{5,21},{6,22},{7,23},{8,24},{9,... | collective-permute-start | bytes 73736 | tf_op jit(solution)/shard_map/ppermute | solution.py:15
  23.9 5.7 %collective-permute-start.5 = (bf16[3,16,256]{2,1,0:T(8,128)(2,1)S(1)}, bf16[3,16,256]{2,1,0:T(8,128)(2,1)S(1)}, u32[]{:S(2)}, u32[]{:S(2)}) collective-permute-start(bf16[3,16,256]{2,1,0:T(8,128)(2,1)S(1)} %get-tuple-element.30), channel_id=1, source_target_pairs={{16,0},{17,1},{18,2},{19,3},{20,4},{21,5},{22,6},{23,7},{24,8},{25... | collective-permute-start | bytes 73736 | tf_op jit(solution)/shard_map/ppermute | solution.py:17
  29.7 6.2 %collective-permute-start.6 = (bf16[22,3,256]{2,1,0:T(4,128)(2,1)S(1)}, bf16[22,3,256]{2,1,0:T(4,128)(2,1)S(1)}, u32[]{:S(2)}, u32[]{:S(2)}) collective-permute-start(bf16[22,3,256]{2,1,0:T(4,128)(2,1)S(1)} %get-tuple-element.21), channel_id=1, source_target_pairs={{0,1},{1,2},{2,3},{3,4},{4,5},{5,6},{6,7},{7,8},{8,9},{9,10},{10,1... | collective-permute-start | bytes 101384 | tf_op jit(solution)/shard_map/ppermute | solution.py:15
  29.8 6.2 %collective-permute-start.7 = (bf16[22,3,256]{2,1,0:T(4,128)(2,1)S(1)}, bf16[22,3,256]{2,1,0:T(4,128)(2,1)S(1)}, u32[]{:S(2)}, u32[]{:S(2)}) collective-permute-start(bf16[22,3,256]{2,1,0:T(4,128)(2,1)S(1)} %get-tuple-element.22), channel_id=1, source_target_pairs={{1,0},{2,1},{3,2},{4,3},{5,4},{6,5},{7,6},{8,7},{9,8},{10,9},{11,1... | collective-permute-start | bytes 101384 | tf_op jit(solution)/shard_map/ppermute | solution.py:17
  38.8 3.1 %collective-permute-start.8 = (bf16[3,16,256]{2,1,0:T(8,128)(2,1)S(1)}, bf16[3,16,256]{2,1,0:T(8,128)(2,1)S(1)}, u32[]{:S(2)}, u32[]{:S(2)}) collective-permute-start(bf16[3,16,256]{2,1,0:T(8,128)(2,1)S(1)} %get-tuple-element.27), channel_id=1, source_target_pairs={{0,16},{1,17},{2,18},{3,19},{4,20},{5,21},{6,22},{7,23},{8,24},{9,... | collective-permute-start | bytes 73736 | tf_op jit(solution)/shard_map/ppermute | solution.py:15
  40.4 5.7 %collective-permute-start.9 = (bf16[3,16,256]{2,1,0:T(8,128)(2,1)S(1)}, bf16[3,16,256]{2,1,0:T(8,128)(2,1)S(1)}, u32[]{:S(2)}, u32[]{:S(2)}) collective-permute-start(bf16[3,16,256]{2,1,0:T(8,128)(2,1)S(1)} %get-tuple-element.28), channel_id=1, source_target_pairs={{16,0},{17,1},{18,2},{19,3},{20,4},{21,5},{22,6},{23,7},{24,8},{25... | collective-permute-start | bytes 73736 | tf_op jit(solution)/shard_map/ppermute | solution.py:17
  46.2 6.2 %collective-permute-start.10 = (bf16[22,3,256]{2,1,0:T(4,128)(2,1)S(1)}, bf16[22,3,256]{2,1,0:T(4,128)(2,1)S(1)}, u32[]{:S(2)}, u32[]{:S(2)}) collective-permute-start(bf16[22,3,256]{2,1,0:T(4,128)(2,1)S(1)} %get-tuple-element.19), channel_id=1, source_target_pairs={{0,1},{1,2},{2,3},{3,4},{4,5},{5,6},{6,7},{7,8},{8,9},{9,10},{10,1... | collective-permute-start | bytes 101384 | tf_op jit(solution)/shard_map/ppermute | solution.py:15
  46.2 6.2 %collective-permute-start.11 = (bf16[22,3,256]{2,1,0:T(4,128)(2,1)S(1)}, bf16[22,3,256]{2,1,0:T(4,128)(2,1)S(1)}, u32[]{:S(2)}, u32[]{:S(2)}) collective-permute-start(bf16[22,3,256]{2,1,0:T(4,128)(2,1)S(1)} %get-tuple-element.20), channel_id=1, source_target_pairs={{1,0},{2,1},{3,2},{4,3},{5,4},{6,5},{7,6},{8,7},{9,8},{10,9},{11,1... | collective-permute-start | bytes 101384 | tf_op jit(solution)/shard_map/ppermute | solution.py:17
  55.2 3.1 %collective-permute-start.12 = (bf16[3,16,256]{2,1,0:T(8,128)(2,1)S(1)}, bf16[3,16,256]{2,1,0:T(8,128)(2,1)S(1)}, u32[]{:S(2)}, u32[]{:S(2)}) collective-permute-start(bf16[3,16,256]{2,1,0:T(8,128)(2,1)S(1)} %get-tuple-element.25), channel_id=1, source_target_pairs={{0,16},{1,17},{2,18},{3,19},{4,20},{5,21},{6,22},{7,23},{8,24},{9,... | collective-permute-start | bytes 73736 | tf_op jit(solution)/shard_map/ppermute | solution.py:15
  56.9 5.7 %collective-permute-start.13 = (bf16[3,16,256]{2,1,0:T(8,128)(2,1)S(1)}, bf16[3,16,256]{2,1,0:T(8,128)(2,1)S(1)}, u32[]{:S(2)}, u32[]{:S(2)}) collective-permute-start(bf16[3,16,256]{2,1,0:T(8,128)(2,1)S(1)} %get-tuple-element.26), channel_id=1, source_target_pairs={{16,0},{17,1},{18,2},{19,3},{20,4},{21,5},{22,6},{23,7},{24,8},{25... | collective-permute-start | bytes 73736 | tf_op jit(solution)/shard_map/ppermute | solution.py:17
  62.6 6.2 %collective-permute-start.14 = (bf16[22,3,256]{2,1,0:T(4,128)(2,1)S(1)}, bf16[22,3,256]{2,1,0:T(4,128)(2,1)S(1)}, u32[]{:S(2)}, u32[]{:S(2)}) collective-permute-start(bf16[22,3,256]{2,1,0:T(4,128)(2,1)S(1)} %get-tuple-element.17), channel_id=1, source_target_pairs={{0,1},{1,2},{2,3},{3,4},{4,5},{5,6},{6,7},{7,8},{8,9},{9,10},{10,1... | collective-permute-start | bytes 101384 | tf_op jit(solution)/shard_map/ppermute | solution.py:15
  62.7 6.2 %collective-permute-start.15 = (bf16[22,3,256]{2,1,0:T(4,128)(2,1)S(1)}, bf16[22,3,256]{2,1,0:T(4,128)(2,1)S(1)}, u32[]{:S(2)}, u32[]{:S(2)}) collective-permute-start(bf16[22,3,256]{2,1,0:T(4,128)(2,1)S(1)} %get-tuple-element.18), channel_id=1, source_target_pairs={{1,0},{2,1},{3,2},{4,3},{5,4},{6,5},{7,6},{8,7},{9,8},{10,9},{11,1... | collective-permute-start | bytes 101384 | tf_op jit(solution)/shard_map/ppermute | solution.py:17
where the time goes:
time: 72.9 us; the launch traced here: 72.3 us
  starting transfers between devices  33.4 us (46%)
  waiting for transfers between devices  19.3 us (26%)
  other arithmetic  9.14 us (13%)
  local copies, waits for them, and re-layouts  6.41 us (9%)
  matrix products  3.69 us (5%)
    ppermute x8, starting transfers between devices, padded_2(): lax.ppermute(head, axis, [((i + 1) % count, i) for i in range(ends)])  23.1 us
    ppermute x8, waiting for transfers between devices, padded_2(): lax.ppermute(head, axis, [((i + 1) % count, i) for i in range(ends)])  12.7 us
    ppermute x8, starting transfers between devices, padded_2(): lax.ppermute(tail, axis, [(i, (i + 1) % count) for i in range(ends)])  10.3 us
    reduce_sum x4, other arithmetic, mixer_rows(): mean_square = jnp.mean(stencil_rows * stencil_rows, axis=-1, keepdims=True)  7.12 us
    ppermute x8, waiting for transfers between devices, padded_2(): lax.ppermute(tail, axis, [(i, (i + 1) % count) for i in range(ends)])  6.58 us
    unnamed x8, local copies, waits for them, and re-layouts  2.12 us
    dot_general x4, matrix products, mixer_rows(): return jnp.dot(hidden, w_second, preferred_element_type=jnp.float32)  1.88 us
    dot_general x4, matrix products, mixer_rows(): jnp.dot(normed, w_first, preferred_element_type=jnp.float32) + b_first  1.82 us
  transfers between devices with their start and end apart: 16, of which 10 were waited for; matrix products, arithmetic and copies ran while one was open for 7% of the time, Pallas kernels for 0%

commit v1 on v0

v1 whole, which is shorter than its diff:
```python
import functools

import jax
import jax.numpy as jnp
import numpy as np
from jax import lax
from jax.experimental import pallas as pl
from jax.experimental.pallas import tpu as pltpu
from jax.sharding import PartitionSpec as P

MESH = pl.DeviceIdType.MESH
LEFT, RIGHT, UP, UP_LEFT, UP_RIGHT, DOWN, DOWN_LEFT, DOWN_RIGHT = range(8)


def row_tables(lat_count, tile_rows):
    total = lat_count * tile_rows
    rows = np.arange(-3, total + 3)
    cosine = np.cos(np.pi * ((rows + 0.5) / total - 0.5))
    cosine = np.where((rows >= 0) & (rows < total), cosine, 0.0)
    table = np.zeros((lat_count, 48), np.float32)
    for i in range(lat_count):
        near = cosine[i * tile_rows : i * tile_rows + tile_rows + 6]
        weight = sum(near[a : a + tile_rows] for a in range(7))
        table[i, : tile_rows + 6] = near
        table[i, 24 : 24 + tile_rows] = 7.0 / weight
    return table


def pick_matrix(tile):
    pick = np.zeros((2, 3 * tile, tile * tile), np.float32)
    for r in range(tile):
        for j in range(3):
            pick[0, 3 * r + j, r * tile + j] = 1.0
            pick[1, 3 * r + j, r * tile + tile - 3 + j] = 1.0
    return pick.reshape(6 * tile, tile * tile)


def place_matrix(tile):
    rows = tile + 6
    place = np.zeros((2, rows * 8, 3 * tile + 32), np.float32)
    for r in range(rows):
        for j in range(3):
            if r < 3:
                source = 7 + 3 * r + j
            elif r < 3 + tile:
                source = 16 + 3 * (r - 3) + j
            else:
                source = 16 + 3 * tile + 3 * (r - 3 - tile) + j
            place[0, r * 8 + 5 + j, source] = 1.0
            place[1, r * 8 + j, source] = 1.0
    return place


def kernel(
    lat_count, lon_count, layers,
    table_s, x_h, mask_h, taps_h, gains_h, w_in_h, b_in_h, w_out_h, pick_h, place_h,
    out_h,
    state, field, part, mask_i, mask_f, cos_v, inv_v, taps, gains, w_in, b_in, w_out, pick, place,
    send_cols, recv_cols, recv_rows, load_sem, w_sem, send_sem, recv_sem,
):
    lat, lon = lax.axis_index("lat"), lax.axis_index("lon")
    left, right = lax.rem(lon + lon_count - 1, lon_count), lax.rem(lon + 1, lon_count)
    has_up, has_down = lat > 0, lat < lat_count - 1

    small = [
        pltpu.make_async_copy(src, dst, load_sem.at[i])
        for i, (src, dst) in enumerate(
            [
                (x_h, state.at[0]), (pick_h, pick), (mask_h, mask_i), (taps_h, taps),
                (place_h, place), (gains_h, gains), (b_in_h, b_in),
            ]
        )
    ]

    def weights(l):
        return (
            pltpu.make_async_copy(w_in_h.at[l], w_in.at[l], w_sem.at[0, l]),
            pltpu.make_async_copy(w_out_h.at[l], w_out.at[l], w_sem.at[1, l]),
        )

    for copy in small:
        copy.start()
    for l in range(layers):
        for copy in weights(l):
            copy.start()

    barrier = pltpu.get_barrier_semaphore()

    def greet(to_lat, to_lon):
        pl.semaphore_signal(barrier, inc=1, device_id=(to_lat, to_lon), device_id_type=MESH)

    greet(lat, left)
    greet(lat, right)

    @pl.when(has_up)
    def _():
        for other in (left, lon, right):
            greet(lat - 1, other)

    @pl.when(has_down)
    def _():
        for other in (left, lon, right):
            greet(lat + 1, other)

    @pl.when(jnp.logical_not(has_up))
    def _():
        recv_cols[:, :, 0:16] = jnp.zeros((layers, 2, 16, 256), jnp.bfloat16)
        recv_rows[:, 0] = jnp.zeros((layers, 3, 16, 256), jnp.bfloat16)

    @pl.when(jnp.logical_not(has_down))
    def _():
        recv_cols[:, :, 64:80] = jnp.zeros((layers, 2, 16, 256), jnp.bfloat16)
        recv_rows[:, 1] = jnp.zeros((layers, 3, 16, 256), jnp.bfloat16)

    for r in range(22):
        cos_v[r] = jnp.full((16, 128), table_s[lat, r], jnp.float32)
    for r in range(16):
        inv_v[r] = jnp.full((8, 128), table_s[lat, 24 + r], jnp.float32)

    small[2].wait()
    eye = lax.broadcasted_iota(jnp.int32, (16, 16), 0) == lax.broadcasted_iota(jnp.int32, (16, 16), 1)
    for r in range(16):
        cells = jnp.where(eye, mask_i[r : r + 1, :].astype(jnp.float32), 0.0)
        mask_f[r] = jnp.broadcast_to(jnp.sum(cells, axis=1, keepdims=True), (16, 128))
    small[0].wait()
    small[1].wait()

    def store_own(rows, cells, first):
        scale = cos_v[3 + first : 3 + first + rows]
        for half in range(2):
            field[half, 3 + first : 3 + first + rows, 8:24, :] = cells[:, :, half * 128 : half * 128 + 128] * scale

    store_own(16, state[0].astype(jnp.float32), 0)

    lats = 1
    for there in (has_up, has_down):
        lats = lats + there.astype(jnp.int32)
    pl.semaphore_wait(barrier, 3 * lats - 1)

    def copies(l):
        def remote(kind, src, dst, to_lat, to_lon):
            return pltpu.make_async_remote_copy(
                src_ref=src, dst_ref=dst, send_sem=send_sem.at[l, kind], recv_sem=recv_sem.at[l, kind],
                device_id=(to_lat, to_lon), device_id_type=MESH,
            )

        def side(kind, s, to_lon):
            return remote(kind, send_cols.at[l, s], recv_cols.at[l, 1 - s, 16:64], lat, to_lon)

        def corner(kind, s, src, dst, to_lat, to_lon):
            return remote(
                kind, send_cols.at[l, s, src : src + 16], recv_cols.at[l, 1 - s, dst : dst + 16], to_lat, to_lon
            )

        sides = [side(LEFT, 0, left), side(RIGHT, 1, right)]
        ups = [
            remote(UP, state.at[l, 0:3], recv_rows.at[l, 1], lat - 1, lon),
            corner(UP_LEFT, 0, 0, 64, lat - 1, left),
            corner(UP_RIGHT, 1, 0, 64, lat - 1, right),
        ]
        downs = [
            remote(DOWN, state.at[l, 13:16], recv_rows.at[l, 0], lat + 1, lon),
            corner(DOWN_LEFT, 0, 32, 0, lat + 1, left),
            corner(DOWN_RIGHT, 1, 32, 0, lat + 1, right),
        ]
        return sides, ups, downs

    def local_columns(g):
        return range(3, 7) if g == 0 else range(0, 4)

    def far_columns(g):
        return range(0, 3) if g == 0 else range(4, 7)

    def layer(l, carry):
        edges = jnp.dot(pick[...], state[l].reshape(256, 256), preferred_element_type=jnp.float32)
        edges = edges.astype(jnp.bfloat16)
        send_cols[l, 0] = edges[0:48]
        send_cols[l, 1] = edges[48:96]
        sides, ups, downs = copies(l)
        for copy in sides:
            copy.start()

        @pl.when(has_up)
        def _():
            for copy in ups:
                copy.start()

        @pl.when(has_down)
        def _():
            for copy in downs:
                copy.start()

        @pl.when(l == 0)
        def _():
            for copy in small[3:]:
                copy.wait()

        def weight(half, a, b):
            lanes = pl.ds(pl.multiple_of(half * 128, 128), 128)
            return taps[l, a, b : b + 1, lanes]

        def near(half, carry):
            for g in range(2):
                acc = jnp.zeros((16, 8, 128), jnp.float32)
                for b in local_columns(g):
                    start = 5 + 8 * g + b
                    x = field[half, 3:19, start : start + 8, :]
                    for a in range(7):
                        low, high = max(0, 3 - a), min(16, 19 - a)
                        add = acc[low:high] + weight(half, a, b) * x[low + a - 3 : high + a - 3]
                        pieces = [acc[:low]] * (low > 0) + [add] + [acc[high:]] * (high < 16)
                        acc = jnp.concatenate(pieces, axis=0) if len(pieces) > 1 else add
                part[half, :, 8 * g : 8 * g + 8, :] = acc
            return carry

        lax.fori_loop(0, 2, near, 0)

        for copy in sides:
            copy.wait_recv()

        @pl.when(has_down)
        def _():
            for copy in ups:
                copy.wait_recv()

        @pl.when(has_up)
        def _():
            for copy in downs:
                copy.wait_recv()

        for s in range(2):
            cells = recv_rows[l, s].astype(jnp.float32)
            scale = cos_v[19 * s : 19 * s + 3]
            columns = jnp.dot(place[s], recv_cols[l, s], preferred_element_type=jnp.float32).reshape(22, 8, 256)
            for half in range(2):
                lanes = slice(half * 128, half * 128 + 128)
                field[half, 19 * s : 19 * s + 3, 8:24, :] = cells[:, :, lanes] * scale
                field[half, :, 24 * s : 24 * s + 8, :] = columns[:, :, lanes] * cos_v[:, 0:8, :]

        def far(half, carry):
            for g in range(2):
                acc = part[half, :, 8 * g : 8 * g + 8, :]
                for b in far_columns(g):
                    start = 5 + 8 * g + b
                    x = field[half, :, start : start + 8, :]
                    for a in range(7):
                        acc = acc + weight(half, a, b) * x[a : a + 16]
                top, mid, low = acc[0:3], acc[3:13], acc[13:16]
                for b in local_columns(g):
                    start = 5 + 8 * g + b
                    above = field[half, 0:3, start : start + 8, :]
                    below = field[half, 19:22, start : start + 8, :]
                    for a in range(3):
                        add = top[0 : 3 - a] + weight(half, a, b) * above[a:3]
                        top = jnp.concatenate([add, top[3 - a :]], axis=0) if a > 0 else add
                    for a in range(4, 7):
                        add = low[6 - a :] + weight(half, a, b) * below[0 : a - 3]
                        low = jnp.concatenate([low[: 6 - a], add], axis=0) if a < 6 else add
                acc = jnp.concatenate([top, mid, low], axis=0) * inv_v[...]
                part[half, :, 8 * g : 8 * g + 8, :] = acc
            return carry

        lax.fori_loop(0, 2, far, 0)

        for copy in weights(l):
            copy.wait()
        gain = gains[pl.ds(l, 1), :]
        bias = b_in[pl.ds(l, 1), :]
        rows = 8
        for block in range(2):
            first = block * rows
            s0 = part[0, first : first + rows].reshape(rows * 16, 128)
            s1 = part[1, first : first + rows].reshape(rows * 16, 128)
            mean = jnp.sum(s0 * s0 + s1 * s1, axis=1, keepdims=True) * (1.0 / 256.0)
            scale = lax.rsqrt(mean + 1e-06)
            normed = jnp.concatenate([s0 * scale * gain[:, :128], s1 * scale * gain[:, 128:]], axis=1)
            half_v = 0.5 * (
                jnp.dot(normed.astype(jnp.bfloat16), w_in[l], preferred_element_type=jnp.float32) + bias
            )
            hidden = (half_v + half_v * jnp.tanh(half_v)).astype(jnp.bfloat16)
            update = jnp.dot(hidden, w_out[l], preferred_element_type=jnp.float32).reshape(rows, 16, 256)
            old = state[l, first : first + rows].astype(jnp.float32)
            wet = mask_f[first : first + rows]
            new = ((old + update) * jnp.concatenate([wet, wet], axis=2)).astype(jnp.bfloat16)
            state[l + 1, first : first + rows] = new
            store_own(rows, new.astype(jnp.float32), first)
        return carry

    lax.fori_loop(0, layers, layer, 0)

    final = pltpu.make_async_copy(state.at[layers], out_h, load_sem.at[7])
    final.start()

    def drain(l, carry):
        sides, ups, downs = copies(l)
        for copy in sides:
            copy.wait_send()

        @pl.when(has_up)
        def _():
            for copy in ups:
                copy.wait_send()

        @pl.when(has_down)
        def _():
            for copy in downs:
                copy.wait_send()

        return carry

    lax.fori_loop(0, layers, drain, 0)
    final.wait()


def local(lat_count, lon_count, ocean_field, ocean_mask, kernels, gains, w_in, b_in, w_out):
    layers = kernels.shape[0]
    bf16, f32 = jnp.bfloat16, jnp.float32
    table = jnp.asarray(row_tables(lat_count, ocean_field.shape[0]))
    pick = jnp.asarray(pick_matrix(16), bf16)
    place = jnp.asarray(place_matrix(16), bf16)
    anywhere = pl.BlockSpec(memory_space=pl.ANY)
    return pl.pallas_call(
        functools.partial(kernel, lat_count, lon_count, layers),
        out_shape=jax.ShapeDtypeStruct(ocean_field.shape, bf16),
        in_specs=[pl.BlockSpec(memory_space=pltpu.SMEM)] + [anywhere] * 9,
        out_specs=anywhere,
        scratch_shapes=[
            pltpu.VMEM((layers + 1, 16, 16, 256), bf16),
            pltpu.VMEM((2, 22, 32, 128), f32),
            pltpu.VMEM((2, 16, 16, 128), f32),
            pltpu.VMEM((16, 16), jnp.int32),
            pltpu.VMEM((16, 16, 128), f32),
            pltpu.VMEM((22, 16, 128), f32),
            pltpu.VMEM((16, 8, 128), f32),
            pltpu.VMEM(kernels.shape, f32),
            pltpu.VMEM(gains.shape, f32),
            pltpu.VMEM(w_in.shape, bf16),
            pltpu.VMEM(b_in.shape, f32),
            pltpu.VMEM(w_out.shape, bf16),
            pltpu.VMEM(pick.shape, bf16),
            pltpu.VMEM(place.shape, bf16),
            pltpu.VMEM((layers, 2, 48, 256), bf16),
            pltpu.VMEM((layers, 2, 80, 256), bf16),
            pltpu.VMEM((layers, 2, 3, 16, 256), bf16),
            pltpu.SemaphoreType.DMA((8,)),
            pltpu.SemaphoreType.DMA((2, layers)),
            pltpu.SemaphoreType.DMA((layers, 8)),
            pltpu.SemaphoreType.DMA((layers, 8)),
        ],
        compiler_params=pltpu.CompilerParams(
            collective_id=0, has_side_effects=True, vmem_limit_bytes=48 * 1024 * 1024
        ),
        cost_estimate=pl.CostEstimate(flops=2200000000, bytes_accessed=5000000, transcendentals=1048576),
    )(table, ocean_field, ocean_mask, kernels, gains, w_in, b_in, w_out, pick, place)


def solution(mesh):
    in_specs = (P("lat", "lon", None), P("lat", "lon"), P(), P(), P(), P(), P())
    out_specs = P("lat", "lon", None)
    body = functools.partial(local, mesh.shape["lat"], mesh.shape["lon"])
    return jax.shard_map(body, mesh=mesh, in_specs=in_specs, out_specs=out_specs, check_vma=False)
```

time: 72.9 us -> 42.9 us (0.59)
  starting transfers between devices: 33.4 us -> 0 us
  Pallas kernels: 0 us -> 32.3 us
  waiting for transfers between devices: 19.3 us -> 0 us
  other arithmetic: 9.14 us -> 0 us
  local copies, waits for them, and re-layouts: 6.41 us -> 10.2 us
  matrix products: 3.69 us -> 0 us
    ppermute x16 -> x0, starting transfers between devices: 33.4 us -> none  [the longest x8 23.1 us: padded_2(): lax.ppermute(head, axis, [((i + 1) % count, i) for i in range(ends)])]
    pallas_call x0 -> x1, Pallas kernels: none -> 32.3 us  [local(): pl.pallas_call(functools.partial(kernel, lat_count, lon_count, layers), o...]
    ppermute x16 -> x0, waiting for transfers between devices: 19.3 us -> none  [the longest x8 12.7 us: padded_2(): lax.ppermute(head, axis, [((i + 1) % count, i) for i in range(ends)])]
    unnamed x8 -> x20, local copies, waits for them, and re-layouts: 2.12 us -> 10.2 us
    reduce_sum x4 -> x0, other arithmetic: 7.12 us -> none  [mixer_rows(): mean_square = jnp.mean(stencil_rows * stencil_rows, axis=-1, keepdims=True)]
    slice x20 -> x0, local copies, waits for them, and re-layouts: 4.25 us -> none  [the longest x1 1.51 us: local(): stencil = metric_conv(padded, kernels[layer_index], cos_near)]
    dot_general x8 -> x0, matrix products: 3.69 us -> none  [the longest x4 1.88 us: mixer_rows(): return jnp.dot(hidden, w_second, preferred_element_type=jnp.float32)]
    convert_element_type x5 -> x0, other arithmetic: 1.25 us -> none  [the longest x1 0.71 us: dense_mix(): wet_mask[..., None].astype(jnp.float32)]
  transfers between devices with their start and end apart: 16 -> 0, of which waited for: 10 -> 0; matrix products, arithmetic and copies ran while one was open for 7% -> 0% of each run, Pallas kernels for 0% -> 0%
where the time goes in v1:
time: 42.9 us; the launch traced here: 42.5 us
  Pallas kernels  32.3 us (75%)
  local copies, waits for them, and re-layouts  10.2 us (24%)
    pallas_call x1, Pallas kernels, local(): pl.pallas_call(functools.partial(kernel, lat_count, lon_count, layers), o...  32.3 us
    unnamed x20, local copies, waits for them, and re-layouts  10.2 us

profile of v1, /device:TPU:0, one launch (start us, length us, event | category | flops | bytes accessed | tf_op | source)
XLA Modules:
  0.0 42.5 jit_solution(18329853564449541955)
XLA Ops:
  0.0 1.0 %copy.11.taps_h = f32[4,7,7,256]{3,2,1,0:T(8,128)S(1)} copy(f32[4,7,7,256]{3,0,2,1:T(4,128)} %param.12) | data formatting | bytes 401408 | tf_op args[2]
  1.0 0.0 copy-start
  1.0 1.6 %copy-done = bf16[4,256,1024]{2,1,0:T(8,128)(2,1)S(1)} copy-done((bf16[4,256,1024]{2,1,0:T(8,128)(2,1)S(1)}, bf16[4,256,1024]{2,1,0:T(8,128)(2,1)}, u32[]{:S(2)}) %copy-start) | copy-done | bytes 2097176
  2.6 0.0 copy-start.1
  2.6 1.6 %copy-done.1 = bf16[4,1024,256]{2,1,0:T(8,128)(2,1)S(1)} copy-done((bf16[4,1024,256]{2,1,0:T(8,128)(2,1)S(1)}, bf16[4,1024,256]{2,1,0:T(8,128)(2,1)}, u32[]{:S(2)}) %copy-start.1) | copy-done | bytes 2097176
  4.2 0.0 copy-start.2
  4.2 0.9 %copy-done.2 = bf16[16,16,256]{2,1,0:T(8,128)(2,1)S(1)} copy-done((bf16[16,16,256]{2,1,0:T(8,128)(2,1)S(1)}, bf16[16,16,256]{2,1,0:T(8,128)(2,1)}, u32[]{:S(2)}) %copy-start.2) | copy-done | bytes 131096
  5.1 0.0 copy-start.3
  5.1 0.7 %copy-done.3 = f32[4,1024]{1,0:T(4,128)S(1)} copy-done((f32[4,1024]{1,0:T(4,128)S(1)}, f32[4,1024]{1,0:T(4,128)}, u32[]{:S(2)}) %copy-start.3) | copy-done | bytes 16408
  5.8 0.0 copy-start.4
  5.8 0.7 %copy-done.4 = s32[16,16]{1,0:T(8,128)S(1)} copy-done((s32[16,16]{1,0:T(8,128)S(1)}, s32[16,16]{1,0:T(8,128)}, u32[]{:S(2)}) %copy-start.4) | copy-done | bytes 1048
  6.5 0.0 copy-start.5
  6.5 0.7 %copy-done.5 = f32[4,256]{1,0:T(4,128)S(1)} copy-done((f32[4,256]{1,0:T(4,128)S(1)}, f32[4,256]{1,0:T(4,128)}, u32[]{:S(2)}) %copy-start.5) | copy-done | bytes 4120
  7.2 0.0 copy-start.6
  7.2 0.9 %copy-done.6 = bf16[2,176,80]{2,1,0:T(8,128)(2,1)S(1)} copy-done((bf16[2,176,80]{2,1,0:T(8,128)(2,1)S(1)}, bf16[2,176,80]{2,1,0:T(8,128)(2,1)}, u32[]{:S(2)}) %copy-start.6) | copy-done | bytes 56344
  8.1 0.0 copy-start.7
  8.1 0.8 %copy-done.7 = bf16[96,256]{1,0:T(8,128)(2,1)S(1)} copy-done((bf16[96,256]{1,0:T(8,128)(2,1)S(1)}, bf16[96,256]{1,0:T(8,128)(2,1)}, u32[]{:S(2)}) %copy-start.7) | copy-done | bytes 49176
  8.9 0.0 copy-start.8
  8.9 0.7 %copy-done.8 = f32[2,48]{1,0:T(2,128)S(1)} copy-done((f32[2,48]{1,0:T(2,128)S(1)}, f32[2,48]{1,0:T(2,128)}, u32[]{:S(2)}) %copy-start.8) | copy-done | bytes 408
  9.5 32.3 %shard_map.100 = bf16[16,16,256]{2,1,0:T(8,128)(2,1)S(1)} custom-call(f32[2,48]{1,0:T(2,128)S(1)} %copy-done.8, bf16[16,16,256]{2,1,0:T(8,128)(2,1)S(1)} %copy-done.2, s32[16,16]{1,0:T(8,128)S(1)} %copy-done.4, f32[4,7,7,256]{3,2,1,0:T(8,128)S(1)} %copy.11.taps_h, f32[4,256]{1,0:T(4,128)S(1)} %copy-done.5, bf16[4,256,1024]{2,1,0:T(8,128)(2,1)S(1)} %copy-done, ...), custom_call_target="tpu_custom_call" | custom-call | flops 2200000000 | bytes 5000000 | tf_op jit(solution)/shard_map/pallas_call | solution.py:322
  41.8 0.7 %copy.13 = bf16[16,16,256]{2,1,0:T(8,128)(2,1)} copy(bf16[16,16,256]{2,1,0:T(8,128)(2,1)S(1)} %shard_map.100) | data formatting | bytes 262144
Async XLA Ops:
  1.0 1.6 %copy-start = (bf16[4,256,1024]{2,1,0:T(8,128)(2,1)S(1)}, bf16[4,256,1024]{2,1,0:T(8,128)(2,1)}, u32[]{:S(2)}) copy-start(bf16[4,256,1024]{2,1,0:T(8,128)(2,1)} %w_in_h.1) | copy-start | bytes 6291460
  2.6 1.6 %copy-start.1 = (bf16[4,1024,256]{2,1,0:T(8,128)(2,1)S(1)}, bf16[4,1024,256]{2,1,0:T(8,128)(2,1)}, u32[]{:S(2)}) copy-start(bf16[4,1024,256]{2,1,0:T(8,128)(2,1)} %w_out_h.1) | copy-start | bytes 6291460
  4.2 0.9 %copy-start.2 = (bf16[16,16,256]{2,1,0:T(8,128)(2,1)S(1)}, bf16[16,16,256]{2,1,0:T(8,128)(2,1)}, u32[]{:S(2)}) copy-start(bf16[16,16,256]{2,1,0:T(8,128)(2,1)} %x_h.1) | copy-start | bytes 393220
  5.1 0.7 %copy-start.3 = (f32[4,1024]{1,0:T(4,128)S(1)}, f32[4,1024]{1,0:T(4,128)}, u32[]{:S(2)}) copy-start(f32[4,1024]{1,0:T(4,128)} %b_in_h.1) | copy-start | bytes 49156
  5.8 0.7 %copy-start.4 = (s32[16,16]{1,0:T(8,128)S(1)}, s32[16,16]{1,0:T(8,128)}, u32[]{:S(2)}) copy-start(s32[16,16]{1,0:T(8,128)} %mask_h.1) | copy-start | bytes 3076
  6.5 0.7 %copy-start.5 = (f32[4,256]{1,0:T(4,128)S(1)}, f32[4,256]{1,0:T(4,128)}, u32[]{:S(2)}) copy-start(f32[4,256]{1,0:T(4,128)} %gains_h.1) | copy-start | bytes 12292
  7.2 0.9 %copy-start.6 = (bf16[2,176,80]{2,1,0:T(8,128)(2,1)S(1)}, bf16[2,176,80]{2,1,0:T(8,128)(2,1)}, u32[]{:S(2)}) copy-start(bf16[2,176,80]{2,1,0:T(8,128)(2,1)} %constant.8.clone.place_h) | copy-start | bytes 168964
  8.1 0.8 %copy-start.7 = (bf16[96,256]{1,0:T(8,128)(2,1)S(1)}, bf16[96,256]{1,0:T(8,128)(2,1)}, u32[]{:S(2)}) copy-start(bf16[96,256]{1,0:T(8,128)(2,1)} %constant.7.clone.pick_h) | copy-start | bytes 147460
  8.9 0.7 %copy-start.8 = (f32[2,48]{1,0:T(2,128)S(1)}, f32[2,48]{1,0:T(2,128)}, u32[]{:S(2)}) copy-start(f32[2,48]{1,0:T(2,128)} %constant.6.clone.table_s) | copy-start | bytes 1156

commit v2 on v1

--- a/solution.py
+++ b/solution.py
@@ -55,7 +55,7 @@
     lat_count, lon_count, layers,
     table_s, x_h, mask_h, taps_h, gains_h, w_in_h, b_in_h, w_out_h, pick_h, place_h,
     out_h,
-    state, field, part, mask_i, mask_f, cos_v, inv_v, taps, gains, w_in, b_in, w_out, pick, place,
+    state, field, part, mask_i, mask_f, cos_v, inv_v, taps, spread, gains, w_in, b_in, w_out, pick, place,
     send_cols, recv_cols, recv_rows, load_sem, w_sem, send_sem, recv_sem,
 ):
     lat, lon = lax.axis_index("lat"), lax.axis_index("lon")
@@ -195,9 +195,19 @@
             for copy in small[3:]:
                 copy.wait()
 
+            def spread_row(a, carry):
+                for b in range(7):
+                    row = taps[a, b]
+                    for at in range(layers):
+                        for half in range(2):
+                            one = row[at : at + 1, half * 128 : half * 128 + 128]
+                            spread[at, half, 7 * a + b] = jnp.broadcast_to(one, (8, 128))
+                return carry
+
+            lax.fori_loop(0, 7, spread_row, 0)
+
         def weight(half, a, b):
-            lanes = pl.ds(pl.multiple_of(half * 128, 128), 128)
-            return taps[l, a, b : b + 1, lanes]
+            return spread[l, half, 7 * a + b]
 
         def near(half, carry):
             for g in range(2):
@@ -318,7 +328,8 @@
     table = jnp.asarray(row_tables(lat_count, ocean_field.shape[0]))
     pick = jnp.asarray(pick_matrix(16), bf16)
     place = jnp.asarray(place_matrix(16), bf16)
-    anywhere = pl.BlockSpec(memory_space=pl.ANY)
+    taps = jnp.transpose(kernels, (1, 2, 0, 3))
+    anywhere = pl.BlockSpec(memory_space=pltpu.HBM)
     return pl.pallas_call(
         functools.partial(kernel, lat_count, lon_count, layers),
         out_shape=jax.ShapeDtypeStruct(ocean_field.shape, bf16),
@@ -332,7 +343,8 @@
             pltpu.VMEM((16, 16, 128), f32),
             pltpu.VMEM((22, 16, 128), f32),
             pltpu.VMEM((16, 8, 128), f32),
-            pltpu.VMEM(kernels.shape, f32),
+            pltpu.VMEM(taps.shape, f32),
+            pltpu.VMEM((layers, 2, 49, 8, 128), f32),
             pltpu.VMEM(gains.shape, f32),
             pltpu.VMEM(w_in.shape, bf16),
             pltpu.VMEM(b_in.shape, f32),
@@ -348,10 +360,10 @@
             pltpu.SemaphoreType.DMA((layers, 8)),
         ],
         compiler_params=pltpu.CompilerParams(
-            collective_id=0, has_side_effects=True, vmem_limit_bytes=48 * 1024 * 1024
+            collective_id=0, has_side_effects=True, vmem_limit_bytes=60 * 1024 * 1024
         ),
         cost_estimate=pl.CostEstimate(flops=2200000000, bytes_accessed=5000000, transcendentals=1048576),
-    )(table, ocean_field, ocean_mask, kernels, gains, w_in, b_in, w_out, pick, place)
+    )(table, ocean_field, ocean_mask, taps, gains, w_in, b_in, w_out, pick, place)
 
 
 def solution(mesh):

time: 42.9 us -> 33.7 us (0.79)
  local copies, waits for them, and re-layouts: 10.2 us -> 1.57 us
    unnamed x20 -> x1, local copies, waits for them, and re-layouts: 10.2 us -> 1.57 us
where the time goes in v2:
time: 33.7 us; the launch traced here: 33.5 us
  Pallas kernels  31.9 us (95%)
  local copies, waits for them, and re-layouts  1.57 us (5%)
    pallas_call x1, Pallas kernels, local(): pl.pallas_call(functools.partial(kernel, lat_count, lon_count, layers), o...  31.9 us
    unnamed x1, local copies, waits for them, and re-layouts  1.57 us

profile of v2, /device:TPU:0, one launch (start us, length us, event | category | flops | bytes accessed | tf_op | source)
XLA Modules:
  0.0 33.5 jit_solution(6594184759749851457)
XLA Ops:
  0.0 31.9 %shard_map.100 = bf16[16,16,256]{2,1,0:T(8,128)(2,1)} custom-call(f32[2,48]{1,0:T(2,128)} %constant.6.clone.table_s, bf16[16,16,256]{2,1,0:T(8,128)(2,1)} %x_h.1, s32[16,16]{1,0:T(8,128)} %mask_h.1, f32[7,7,4,256]{3,2,1,0:T(4,128)} %bitcast.1, f32[4,256]{1,0:T(4,128)} %gains_h.1, bf16[4,256,1024]{2,1,0:T(8,128)(2,1)} %w_in_h.1, f32[4,1024]{1,0:T(4,128)} %b_in_h.1, ...), custom_call_target="tpu_custom_call" | custom-call | flops 2200000000 | bytes 5000000 | tf_op jit(solution)/shard_map/pallas_call | solution.py:333
  32.0 1.6 %copy.12 = bf16[16,16,256]{2,1,0:T(8,128)(2,1)} copy(bf16[16,16,256]{2,1,0:T(8,128)(2,1)} %shard_map.100) | data formatting | bytes 262144

commit v3 on v2

v3 whole, which is shorter than its diff:
```python
import functools

import jax
import jax.numpy as jnp
import numpy as np
from jax import lax
from jax.experimental import pallas as pl
from jax.experimental.pallas import tpu as pltpu
from jax.sharding import PartitionSpec as P

MESH = pl.DeviceIdType.MESH
LEFT, RIGHT, UP, UP_LEFT, UP_RIGHT, DOWN, DOWN_LEFT, DOWN_RIGHT = range(8)


def row_tables(lat_count, tile_rows):
    total = lat_count * tile_rows
    rows = np.arange(-6, total + 6)
    cosine = np.cos(np.pi * ((rows + 0.5) / total - 0.5))
    cosine = np.where((rows >= 0) & (rows < total), cosine, 0.0)
    table = np.zeros((lat_count, 64), np.float32)
    for i in range(lat_count):
        near = cosine[i * tile_rows : i * tile_rows + tile_rows + 12]
        weight = sum(near[a : a + tile_rows + 6] for a in range(7))
        table[i, : tile_rows + 12] = near
        table[i, 32 : 32 + tile_rows + 6] = 7.0 / weight
    return table


def pick_matrix(tile):
    pick = np.zeros((2, 6 * tile, tile * tile), np.float32)
    for r in range(tile):
        for j in range(6):
            pick[0, 6 * r + j, r * tile + j] = 1.0
            pick[1, 6 * r + j, r * tile + tile - 6 + j] = 1.0
    return pick.reshape(12 * tile, tile * tile)


def place_matrix(tile):
    rows = tile + 12
    place = np.zeros((2, rows * 8, 6 * tile + 96), np.float32)
    for r in range(rows):
        for j in range(6):
            if r < 6:
                source = 12 + 6 * r + j
            elif r < 6 + tile:
                source = 48 + 6 * (r - 6) + j
            else:
                source = 48 + 6 * tile + 6 * (r - 6 - tile) + j
            place[0, r * 8 + 2 + j, source] = 1.0
            place[1, r * 8 + j, source] = 1.0
    return place


def kernel(
    lat_count, lon_count, layers,
    table_s, x_h, mask_h, taps_h, gains_h, w_in_h, b_in_h, w_out_h, pick_h, place_h,
    out_h,
    state_0, state_1, final, field, plain, part, mask_i, wet, cos_v, inv_v, taps, spread, gains, w_in, b_in,
    w_out, pick, place,
    cols_out_0, cols_out_1, cols_in_0, cols_in_1, rows_in_0, rows_in_1, load_sem, w_sem, send_sem, recv_sem,
):
    lat, lon = lax.axis_index("lat"), lax.axis_index("lon")
    left, right = lax.rem(lon + lon_count - 1, lon_count), lax.rem(lon + 1, lon_count)
    has_up, has_down = lat > 0, lat < lat_count - 1
    state, cols_out = (state_0, state_1), (cols_out_0, cols_out_1)
    cols_in, rows_in = (cols_in_0, cols_in_1), (rows_in_0, rows_in_1)

    small = [
        pltpu.make_async_copy(src, dst, load_sem.at[i])
        for i, (src, dst) in enumerate(
            [
                (x_h, final), (pick_h, pick), (mask_h, mask_i), (taps_h, taps),
                (place_h, place), (gains_h, gains), (b_in_h, b_in),
            ]
        )
    ]

    def weights(l):
        return (
            pltpu.make_async_copy(w_in_h.at[l], w_in.at[l], w_sem.at[0, l]),
            pltpu.make_async_copy(w_out_h.at[l], w_out.at[l], w_sem.at[1, l]),
        )

    for copy in small:
        copy.start()
    for l in range(layers):
        for copy in weights(l):
            copy.start()

    barrier = pltpu.get_barrier_semaphore()

    def greet(to_lat, to_lon):
        pl.semaphore_signal(barrier, inc=1, device_id=(to_lat, to_lon), device_id_type=MESH)

    greet(lat, left)
    greet(lat, right)

    @pl.when(has_up)
    def _():
        for other in (left, lon, right):
            greet(lat - 1, other)

    @pl.when(has_down)
    def _():
        for other in (left, lon, right):
            greet(lat + 1, other)

    @pl.when(jnp.logical_not(has_up))
    def _():
        for p in range(2):
            width = cols_in[p].shape[2]
            cols_in[p][:, 0:48] = jnp.zeros((2, 48, width), jnp.bfloat16)
            rows_in[p][0] = jnp.zeros((6, 16, width), jnp.bfloat16)

    @pl.when(jnp.logical_not(has_down))
    def _():
        for p in range(2):
            width = cols_in[p].shape[2]
            cols_in[p][:, 144:192] = jnp.zeros((2, 48, width), jnp.bfloat16)
            rows_in[p][1] = jnp.zeros((6, 16, width), jnp.bfloat16)

    for r in range(28):
        cos_v[r] = jnp.full((8, 128), table_s[lat, r], jnp.float32)
    for r in range(22):
        inv_v[r] = jnp.full((8, 128), table_s[lat, 32 + r], jnp.float32)

    small[2].wait()
    eye = lax.broadcasted_iota(jnp.int32, (16, 16), 0) == lax.broadcasted_iota(jnp.int32, (16, 16), 1)
    for r in range(16):
        cells = jnp.where(eye, mask_i[r : r + 1, :].astype(jnp.float32), 0.0)
        cells = jnp.broadcast_to(jnp.sum(cells, axis=1, keepdims=True), (16, 128))
        wet[6 + r, 8:24, :] = cells
        state_0[r, :, 256:384] = cells.astype(jnp.bfloat16)
    small[0].wait()
    state_0[:, :, 0:256] = final[...]
    small[1].wait()

    def store(row, rows, column, columns, cells):
        scale = jnp.concatenate([cos_v[row : row + rows]] * (columns // 8), axis=1)
        for half in range(2):
            values = cells[:, :, half * 128 : half * 128 + 128]
            plain[half, row : row + rows, column : column + columns, :] = values
            field[half, row : row + rows, column : column + columns, :] = values * scale

    lats = 1
    for there in (has_up, has_down):
        lats = lats + there.astype(jnp.int32)
    pl.semaphore_wait(barrier, 3 * lats - 1)

    def copies(p):
        def remote(kind, src, dst, to_lat, to_lon):
            return pltpu.make_async_remote_copy(
                src_ref=src, dst_ref=dst, send_sem=send_sem.at[p, kind], recv_sem=recv_sem.at[p, kind],
                device_id=(to_lat, to_lon), device_id_type=MESH,
            )

        def side(kind, s, to_lon):
            return remote(kind, cols_out[p].at[s], cols_in[p].at[1 - s, 48:144], lat, to_lon)

        def corner(kind, s, src, dst, to_lat, to_lon):
            return remote(
                kind, cols_out[p].at[s, src : src + 48], cols_in[p].at[1 - s, dst : dst + 48], to_lat, to_lon
            )

        sides = [side(LEFT, 0, left), side(RIGHT, 1, right)]
        ups = [
            corner(UP_LEFT, 0, 0, 144, lat - 1, left),
            corner(UP_RIGHT, 1, 0, 144, lat - 1, right),
            remote(UP, state[p].at[0:6], rows_in[p].at[1], lat - 1, lon),
        ]
        downs = [
            corner(DOWN_LEFT, 0, 48, 0, lat + 1, left),
            corner(DOWN_RIGHT, 1, 48, 0, lat + 1, right),
            remote(DOWN, state[p].at[10:16], rows_in[p].at[0], lat + 1, lon),
        ]
        return sides, ups, downs

    def taps_over(l, half, acc, start, first, rows):
        for b in range(7):
            x = field[half, first : first + rows + 6, start - 3 + b : start + 5 + b, :]
            for a in range(7):
                acc = acc + spread[l, half, 7 * a + b] * x[a : a + rows]
        return acc

    def mix(l, rows, first_row, column, columns, block_rows, emit):
        for copy in weights(l):
            copy.wait()
        gain, bias = gains[l : l + 1, :], b_in[l : l + 1, :]
        for first in range(0, rows, block_rows):
            cells = block_rows * columns
            s0 = part[0, first : first + block_rows, 0:columns].reshape(cells, 128)
            s1 = part[1, first : first + block_rows, 0:columns].reshape(cells, 128)
            mean = jnp.sum(s0 * s0 + s1 * s1, axis=1, keepdims=True) * (1.0 / 256.0)
            scale = lax.rsqrt(mean + 1e-06)
            normed = jnp.concatenate([s0 * scale * gain[:, :128], s1 * scale * gain[:, 128:]], axis=1)
            half_v = 0.5 * (
                jnp.dot(normed.astype(jnp.bfloat16), w_in[l], preferred_element_type=jnp.float32) + bias
            )
            hidden = (half_v + half_v * jnp.tanh(half_v)).astype(jnp.bfloat16)
            update = jnp.dot(hidden, w_out[l], preferred_element_type=jnp.float32)
            update = update.reshape(block_rows, columns, 256)
            row = first_row + first
            here = (slice(row, row + block_rows), slice(column, column + columns))
            old = jnp.concatenate([plain[(0, *here)], plain[(1, *here)]], axis=2)
            dry = wet[here]
            new = (old + update) * jnp.concatenate([dry, dry], axis=2)
            emit(row, new.astype(jnp.bfloat16))

    for p in range(2):
        l = 2 * p
        edges = jnp.dot(
            pick[...], state[p][...].reshape(256, state[p].shape[2]), preferred_element_type=jnp.float32
        ).astype(jnp.bfloat16)
        cols_out[p][0] = edges[0:96]
        cols_out[p][1] = edges[96:192]
        sides, ups, downs = copies(p)

        @pl.when(has_up)
        def _(ups=ups):
            for copy in ups:
                copy.start()

        @pl.when(has_down)
        def _(downs=downs):
            for copy in downs:
                copy.start()

        for copy in sides:
            copy.start()

        if p == 0:
            store(6, 16, 8, 16, state[0][:, :, 0:256].astype(jnp.float32))
            for copy in small[3:]:
                copy.wait()

            def spread_row(a, carry):
                for b in range(7):
                    row = taps[a, b]
                    for at in range(layers):
                        for half in range(2):
                            one = row[at : at + 1, half * 128 : half * 128 + 128]
                            spread[at, half, 7 * a + b] = jnp.broadcast_to(one, (8, 128))
                return carry

            lax.fori_loop(0, 7, spread_row, 0)

        def near(half, carry, l=l):
            acc = jnp.zeros((22, 8, 128), jnp.float32)
            for b in range(7):
                x = field[half, 6:22, 10 + b : 18 + b, :]
                for a in range(7):
                    low, high = max(0, 6 - a), 22 - a
                    add = acc[low:high] + spread[l, half, 7 * a + b] * x[low + a - 6 : high + a - 6]
                    pieces = [acc[:low]] * (low > 0) + [add] + [acc[high:]] * (high < 22)
                    acc = jnp.concatenate(pieces, axis=0)
            part[half, :, 8:16, :] = acc
            return carry

        lax.fori_loop(0, 2, near, 0)

        for copy in sides:
            copy.wait_recv()

        @pl.when(has_down)
        def _(ups=ups):
            for copy in ups:
                copy.wait_recv()

        @pl.when(has_up)
        def _(downs=downs):
            for copy in downs:
                copy.wait_recv()

        for s in range(2):
            cells = rows_in[p][s].astype(jnp.float32)
            columns = jnp.dot(place[s], cols_in[p][s], preferred_element_type=jnp.float32)
            columns = columns.reshape(28, 8, cols_in[p].shape[2])
            store(22 * s, 6, 8, 16, cells[:, :, 0:256])
            store(0, 28, 24 * s, 8, columns[:, :, 0:256])
            if p == 0:
                wet[22 * s : 22 * s + 6, 8:24, :] = cells[:, :, 256:384]
                wet[:, 24 * s : 24 * s + 8, :] = columns[:, :, 256:384]

        def far(half, carry, l=l):
            acc = part[half, :, 8:16, :]
            top, mid, low = acc[0:6], acc[6:16], acc[16:22]
            for b in range(7):
                above = field[half, 0:6, 10 + b : 18 + b, :]
                below = field[half, 22:28, 10 + b : 18 + b, :]
                for a in range(6):
                    add = top[0 : 6 - a] + spread[l, half, 7 * a + b] * above[a:6]
                    top = jnp.concatenate([add, top[6 - a :]], axis=0) if a > 0 else add
                for a in range(1, 7):
                    add = low[6 - a :] + spread[l, half, 7 * a + b] * below[0:a]
                    low = jnp.concatenate([low[: 6 - a], add], axis=0) if a < 6 else add
            part[half, :, 8:16, :] = jnp.concatenate([top, mid, low], axis=0) * inv_v[...]
            for g in (0, 2):
                acc = taps_over(l, half, jnp.zeros((22, 8, 128), jnp.float32), 5 + 8 * g, 0, 22)
                part[half, :, 8 * g : 8 * g + 8, :] = acc * inv_v[...]
            return carry

        lax.fori_loop(0, 2, far, 0)

        def emit_wide(row, new):
            store(row, new.shape[0], 5, 24, new.astype(jnp.float32))

        mix(l, 22, 3, 5, 24, 11, emit_wide)

        def own(half, carry, l=l):
            for g in range(2):
                acc = taps_over(l + 1, half, jnp.zeros((16, 8, 128), jnp.float32), 8 + 8 * g, 3, 16)
                part[half, 0:16, 8 * g : 8 * g + 8, :] = acc * inv_v[3:19]
            return carry

        lax.fori_loop(0, 2, own, 0)

        def emit_own(row, new, p=p):
            if p == 0:
                state_1[row - 6 : row - 6 + new.shape[0]] = new
                store(row, new.shape[0], 8, 16, new.astype(jnp.float32))
            else:
                final[row - 6 : row - 6 + new.shape[0]] = new

        mix(l + 1, 16, 6, 8, 16, 8, emit_own)

    result = pltpu.make_async_copy(final, out_h, load_sem.at[7])
    result.start()

    for p in range(2):
        sides, ups, downs = copies(p)
        for copy in sides:
            copy.wait_send()

        @pl.when(has_up)
        def _(ups=ups):
            for copy in ups:
                copy.wait_send()

        @pl.when(has_down)
        def _(downs=downs):
            for copy in downs:
                copy.wait_send()

    result.wait()


def local(lat_count, lon_count, ocean_field, ocean_mask, kernels, gains, w_in, b_in, w_out):
    layers = kernels.shape[0]
    bf16, f32 = jnp.bfloat16, jnp.float32
    table = jnp.asarray(row_tables(lat_count, ocean_field.shape[0]))
    pick = jnp.asarray(pick_matrix(16), bf16)
    place = jnp.asarray(place_matrix(16), bf16)
    taps = jnp.transpose(kernels, (1, 2, 0, 3))
    anywhere = pl.BlockSpec(memory_space=pltpu.HBM)
    return pl.pallas_call(
        functools.partial(kernel, lat_count, lon_count, layers),
        out_shape=jax.ShapeDtypeStruct(ocean_field.shape, bf16),
        in_specs=[pl.BlockSpec(memory_space=pltpu.SMEM)] + [anywhere] * 9,
        out_specs=anywhere,
        scratch_shapes=[
            pltpu.VMEM((16, 16, 384), bf16),
            pltpu.VMEM((16, 16, 256), bf16),
            pltpu.VMEM((16, 16, 256), bf16),
            pltpu.VMEM((2, 28, 32, 128), f32),
            pltpu.VMEM((2, 28, 32, 128), f32),
            pltpu.VMEM((2, 22, 24, 128), f32),
            pltpu.VMEM((16, 16), jnp.int32),
            pltpu.VMEM((28, 32, 128), f32),
            pltpu.VMEM((28, 8, 128), f32),
            pltpu.VMEM((22, 8, 128), f32),
            pltpu.VMEM(taps.shape, f32),
            pltpu.VMEM((layers, 2, 49, 8, 128), f32),
            pltpu.VMEM(gains.shape, f32),
            pltpu.VMEM(w_in.shape, bf16),
            pltpu.VMEM(b_in.shape, f32),
            pltpu.VMEM(w_out.shape, bf16),
            pltpu.VMEM(pick.shape, bf16),
            pltpu.VMEM(place.shape, bf16),
            pltpu.VMEM((2, 96, 384), bf16),
            pltpu.VMEM((2, 96, 256), bf16),
            pltpu.VMEM((2, 192, 384), bf16),
            pltpu.VMEM((2, 192, 256), bf16),
            pltpu.VMEM((2, 6, 16, 384), bf16),
            pltpu.VMEM((2, 6, 16, 256), bf16),
            pltpu.SemaphoreType.DMA((8,)),
            pltpu.SemaphoreType.DMA((2, layers)),
            pltpu.SemaphoreType.DMA((2, 8)),
            pltpu.SemaphoreType.DMA((2, 8)),
        ],
        compiler_params=pltpu.CompilerParams(
            collective_id=0, has_side_effects=True, vmem_limit_bytes=60 * 1024 * 1024
        ),
        cost_estimate=pl.CostEstimate(flops=2200000000, bytes_accessed=5000000, transcendentals=1048576),
    )(table, ocean_field, ocean_mask, taps, gains, w_in, b_in, w_out, pick, place)


def solution(mesh):
    in_specs = (P("lat", "lon", None), P("lat", "lon"), P(), P(), P(), P(), P())
    out_specs = P("lat", "lon", None)
    body = functools.partial(local, mesh.shape["lat"], mesh.shape["lon"])
    return jax.shard_map(body, mesh=mesh, in_specs=in_specs, out_specs=out_specs, check_vma=False)
```

time: 33.7 us -> 29.9 us (0.89)
  Pallas kernels: 31.9 us -> 28.2 us
    pallas_call x1, Pallas kernels: 31.9 us -> 28.2 us  [local(): pl.pallas_call(functools.partial(kernel, lat_count, lon_count, layers), o...]
where the time goes in v3:
time: 29.9 us; the launch traced here: 29.7 us
  Pallas kernels  28.2 us (94%)
  local copies, waits for them, and re-layouts  1.57 us (5%)
    pallas_call x1, Pallas kernels, local(): pl.pallas_call(functools.partial(kernel, lat_count, lon_count, layers), o...  28.2 us
    unnamed x1, local copies, waits for them, and re-layouts  1.57 us

profile of v3, /device:TPU:0, one launch (start us, length us, event | category | flops | bytes accessed | tf_op | source)
XLA Modules:
  0.0 29.7 jit_solution(13306835779884330451)
XLA Ops:
  0.0 28.2 %shard_map.100 = bf16[16,16,256]{2,1,0:T(8,128)(2,1)} custom-call(f32[2,64]{1,0:T(2,128)} %constant.6.clone.table_s, bf16[16,16,256]{2,1,0:T(8,128)(2,1)} %x_h.1, s32[16,16]{1,0:T(8,128)} %mask_h.1, f32[7,7,4,256]{3,2,1,0:T(4,128)} %bitcast.1, f32[4,256]{1,0:T(4,128)} %gains_h.1, bf16[4,256,1024]{2,1,0:T(8,128)(2,1)} %w_in_h.1, f32[4,1024]{1,0:T(4,128)} %b_in_h.1, ...), custom_call_target="tpu_custom_call" | custom-call | flops 2200000000 | bytes 5000000 | tf_op jit(solution)/shard_map/pallas_call | solution.py:355
  28.2 1.6 %copy.12 = bf16[16,16,256]{2,1,0:T(8,128)(2,1)} copy(bf16[16,16,256]{2,1,0:T(8,128)(2,1)} %shard_map.100) | data formatting | bytes 262144

commit v4 on v3

--- a/solution.py
+++ b/solution.py
@@ -208,28 +208,37 @@
 
     for p in range(2):
         l = 2 * p
+        sides, ups, downs = copies(p)
+
+        @pl.when(has_up)
+        def _(ups=ups):
+            ups[2].start()
+
+        @pl.when(has_down)
+        def _(downs=downs):
+            downs[2].start()
+
         edges = jnp.dot(
             pick[...], state[p][...].reshape(256, state[p].shape[2]), preferred_element_type=jnp.float32
         ).astype(jnp.bfloat16)
         cols_out[p][0] = edges[0:96]
         cols_out[p][1] = edges[96:192]
-        sides, ups, downs = copies(p)
 
         @pl.when(has_up)
         def _(ups=ups):
-            for copy in ups:
+            for copy in ups[:2]:
                 copy.start()
 
         @pl.when(has_down)
         def _(downs=downs):
-            for copy in downs:
+            for copy in downs[:2]:
                 copy.start()
 
         for copy in sides:
             copy.start()
 
+        store(6, 16, 8, 16, state[p][:, :, 0:256].astype(jnp.float32))
         if p == 0:
-            store(6, 16, 8, 16, state[0][:, :, 0:256].astype(jnp.float32))
             for copy in small[3:]:
                 copy.wait()
 
@@ -304,7 +313,7 @@
         def emit_wide(row, new):
             store(row, new.shape[0], 5, 24, new.astype(jnp.float32))
 
-        mix(l, 22, 3, 5, 24, 11, emit_wide)
+        mix(l, 22, 3, 5, 24, 22, emit_wide)
 
         def own(half, carry, l=l):
             for g in range(2):
@@ -317,11 +326,10 @@
         def emit_own(row, new, p=p):
             if p == 0:
                 state_1[row - 6 : row - 6 + new.shape[0]] = new
-                store(row, new.shape[0], 8, 16, new.astype(jnp.float32))
             else:
                 final[row - 6 : row - 6 + new.shape[0]] = new
 
-        mix(l + 1, 16, 6, 8, 16, 8, emit_own)
+        mix(l + 1, 16, 6, 8, 16, 16, emit_own)
 
     result = pltpu.make_async_copy(final, out_h, load_sem.at[7])
     result.start()

time: 29.9 us -> 29.9 us (level)
  no operation moved by 1% of the time
where the time goes in v4:
time: 29.9 us; the launch traced here: 29.7 us
  Pallas kernels  28.2 us (94%)
  local copies, waits for them, and re-layouts  1.57 us (5%)
    pallas_call x1, Pallas kernels, local(): pl.pallas_call(functools.partial(kernel, lat_count, lon_count, layers), o...  28.2 us
    unnamed x1, local copies, waits for them, and re-layouts  1.57 us

profile of v4, /device:TPU:0, one launch (start us, length us, event | category | flops | bytes accessed | tf_op | source)
XLA Modules:
  0.0 29.7 jit_solution(8786254644168207983)
XLA Ops:
  0.0 28.2 %shard_map.100 = bf16[16,16,256]{2,1,0:T(8,128)(2,1)} custom-call(f32[2,64]{1,0:T(2,128)} %constant.6.clone.table_s, bf16[16,16,256]{2,1,0:T(8,128)(2,1)} %x_h.1, s32[16,16]{1,0:T(8,128)} %mask_h.1, f32[7,7,4,256]{3,2,1,0:T(4,128)} %bitcast.1, f32[4,256]{1,0:T(4,128)} %gains_h.1, bf16[4,256,1024]{2,1,0:T(8,128)(2,1)} %w_in_h.1, f32[4,1024]{1,0:T(4,128)} %b_in_h.1, ...), custom_call_target="tpu_custom_call" | custom-call | flops 2200000000 | bytes 5000000 | tf_op jit(solution)/shard_map/pallas_call | solution.py:363
  28.2 1.6 %copy.12 = bf16[16,16,256]{2,1,0:T(8,128)(2,1)} copy(bf16[16,16,256]{2,1,0:T(8,128)(2,1)} %shard_map.100) | data formatting | bytes 262144
